TPU v7x, 256 devices: a whole 4x4x8 slice. The times are simulated.
256 devices in a mesh: term: 16 (over z, y_hi), sector: 16 (over x, y_lo, core).
Axes of the slice: x: 4, y: 4 (y_hi: 2, y_lo: 2; y = y_hi * 2 + y_lo), z: 8, core: 2. Of those that a mesh axis runs over, the one named last changes fastest.
Arguments:
- psi: bfloat16 [64, 128, 128], P('sector', 'term'), may hold values from -75 to 75
- diag_energy: float32 [64, 128, 128], P('sector', 'term'), may hold values from -4 to 6
- block_shape: int32 [64, 2], P('sector'), may hold values from 32 to 128
- env_left: bfloat16 [16, 16, 32, 128, 128], P('term', 'sector'), may hold values from -0.5 to 0.5
- env_right: bfloat16 [16, 16, 32, 128, 128], P('term', 'sector'), may hold values from -0.5 to 0.5
- pair_src: int32 [16, 16, 384], P('term', 'sector'), may hold values from 0 to 63
- pair_dst: int32 [16, 16, 384], P('term', 'sector'), may hold values from 0 to 3
- pair_left: int32 [16, 16, 384], P('term', 'sector'), may hold values from 0 to 31
- pair_right: int32 [16, 16, 384], P('term', 'sector'), may hold values from 0 to 31
- pair_count: int32 [16, 16], P('term', 'sector'), may hold values from 48 to 384, as said below
Outputs:
- sigma_one: float32 [64, 128, 128], P('sector', 'term')
- sigma_two: float32 [64, 128, 128], P('sector', 'term')
Inputs may be any that keep to these rules, and one draw needn't show every extreme that they name: The live slots of the device at term index t and sector index s are slots 0 to pair_count[t, s] - 1; some device has all 384 slots live. A slot of sector index s adds to the global block s * 4 + pair_dst.
All inputs are finite; a program needn't handle non-finite values.
Results may differ from a plain program's by a relative error of at most 0.006.
Values may be sent and summed in bfloat16 or wider, within the bound.
A program may use at most 64 MiB of HBM per device.

v0:
```python
import jax
import jax.numpy as jnp
from jax import lax
from jax.sharding import PartitionSpec as P


def region(block_shape, row_ids, tile_width):
    col_ids = jnp.arange(tile_width, dtype=jnp.int32)
    return (row_ids[None, :, None] < block_shape[:, 0, None, None]) & (
        col_ids[None, None, :] < block_shape[:, 1, None, None]
    )


def collect(vector_here):
    whole_rows = lax.all_gather(vector_here, "term", axis=1, tiled=True)
    return lax.all_gather(whole_rows, "sector", axis=0, tiled=True)


def contract(
    full_vector,
    left_tiles,
    right_tiles,
    source_ids,
    target_ids,
    left_ids,
    right_ids,
    live_count,
    blocks_here,
):
    group_size = 16
    tile_width = full_vector.shape[1]
    rounds = (live_count + group_size - 1) // group_size
    block_ids = jnp.arange(blocks_here, dtype=jnp.int32)
    slot_ids = jnp.arange(group_size, dtype=jnp.int32)

    def accumulate(turn_index, running):
        begin = turn_index * group_size
        source_part = lax.dynamic_slice_in_dim(source_ids, begin, group_size)
        target_part = lax.dynamic_slice_in_dim(target_ids, begin, group_size)
        left_part = lax.dynamic_slice_in_dim(left_ids, begin, group_size)
        right_part = lax.dynamic_slice_in_dim(right_ids, begin, group_size)
        moved = jnp.take(full_vector, source_part, axis=0)
        left_ops = jnp.take(left_tiles, left_part, axis=0)
        right_ops = jnp.take(right_tiles, right_part, axis=0)
        left_half = jnp.einsum(
            "pxk,pky->pxy", left_ops, moved, preferred_element_type=jnp.float32
        ).astype(jnp.bfloat16)
        product = jnp.einsum(
            "pxk,pky->pxy", left_half, right_ops, preferred_element_type=jnp.float32
        )
        live_slots = (begin + slot_ids < live_count).astype(jnp.float32)
        onehot = (target_part[:, None] == block_ids[None, :]).astype(jnp.float32) * live_slots[
            :, None
        ]
        return running + jnp.einsum("pb,pxy->bxy", onehot, product)

    initial = jnp.zeros((blocks_here, tile_width, tile_width), jnp.float32)
    return lax.fori_loop(0, rounds, accumulate, initial)


def reduce_split(partial_sums):
    return lax.psum_scatter(partial_sums, "term", scatter_dimension=1, tiled=True)


def body(
    psi,
    diag_energy,
    block_shape,
    env_left,
    env_right,
    pair_src,
    pair_dst,
    pair_left,
    pair_right,
    pair_count,
):
    blocks_here, rows_here, tile_width = psi.shape
    row_start = lax.axis_index("term") * rows_here
    entries = lax.axis_size("sector") * blocks_here * tile_width * tile_width
    row_ids = row_start + jnp.arange(rows_here, dtype=jnp.int32)
    inside_here = region(block_shape, row_ids, tile_width)
    start_here = jnp.where(inside_here, psi, jnp.zeros_like(psi))
    left_tiles = env_left[0, 0]
    right_tiles = env_right[0, 0]
    source_ids = pair_src[0, 0]
    target_ids = pair_dst[0, 0]
    left_ids = pair_left[0, 0]
    right_ids = pair_right[0, 0]
    live_count = pair_count[0, 0]
    full_start = collect(start_here)
    term_sums = contract(
        full_start,
        left_tiles,
        right_tiles,
        source_ids,
        target_ids,
        left_ids,
        right_ids,
        live_count,
        blocks_here,
    )
    start_float = start_here.astype(jnp.float32)
    sigma_one = jnp.where(
        inside_here, diag_energy * start_float + reduce_split(term_sums), jnp.float32(0.0)
    )
    correlation, squared = lax.psum(
        (jnp.sum(start_float * sigma_one), jnp.sum(start_float * start_float)), ("term", "sector")
    )
    rayleigh = correlation / squared
    residual = sigma_one - rayleigh * start_float
    resid_total = lax.psum(jnp.sum(residual * residual), ("term", "sector"))
    second_here = (residual * lax.rsqrt(resid_total / entries + 1e-06)).astype(jnp.bfloat16)
    full_second = collect(second_here)
    second_sums = contract(
        full_second,
        left_tiles,
        right_tiles,
        source_ids,
        target_ids,
        left_ids,
        right_ids,
        live_count,
        blocks_here,
    )
    sigma_two = jnp.where(
        inside_here,
        diag_energy * second_here.astype(jnp.float32) + reduce_split(second_sums),
        jnp.float32(0.0),
    )
    return (sigma_one, sigma_two)


def solution(mesh):
    placed = (
        P("sector", "term", None),
        P("sector", "term", None),
        P("sector", None),
        P("term", "sector", None, None, None),
        P("term", "sector", None, None, None),
        P("term", "sector", None),
        P("term", "sector", None),
        P("term", "sector", None),
        P("term", "sector", None),
        P("term", "sector"),
    )
    return jax.shard_map(
        body,
        mesh=mesh,
        in_specs=placed,
        out_specs=(P("sector", "term", None), P("sector", "term", None)),
        check_vma=False,
    )
```

profile of v0, /device:TPU:1, one launch (start us, length us, event | category | flops | bytes accessed | tf_op | source)
XLA Modules:
  0.0 1055.3 jit_solution(7568392855414453714)
XLA Ops:
  8.9 40.9 %all_gather.12 = bf16[4,128,128]{2,1,0:T(8,128)(2,1)} all-gather(bf16[4,8,128]{2,1,0:T(8,128)(2,1)S(1)} %and_select_fusion.2), channel_id=1, replica_groups=mesh['term'=16,'sector'=16] {'term'}, dimensions={1}, use_global_device_ids=true | all-gather | bytes 139264 | tf_op jit(solution)/shard_map/all_gather | solution.py:15
  53.4 36.0 %all-gather.3.cloned.1.call-done = bf16[64,128,128]{2,1,0:T(8,128)(2,1)} async-done(((bf16[4,128,128]{2,1,0:T(8,128)(2,1)}), bf16[64,128,128]{2,1,0:T(8,128)(2,1)}) %all-gather.3.cloned.1.call-update) | async-done | bytes 2097168 | tf_op jit(solution)/shard_map/all_gather | solution.py:16
  89.5 63.2 %while.22 = (s32[]{:T(128)}, f32[4,128,128]{2,0,1:T(4,128)S(1)}, s32[]{:T(128)}, s32[384]{0:T(512)S(1)}, s32[]{:T(128)}, /*index=5*/s32[384]{0:T(512)S(1)}, bf16...) while((s32[]{:T(128)}, f32[4,128,128]{2,0,1:T(4,128)S(1)}, ...), condition=%wide.region_1.4_spmd.clone, body=%wide.region_0.3_spmd.clone.sunk | while | flops 137432528 | bytes 10499403 | solution.py:58
  89.6 0.8 compare_and_fusion.11
  90.5 2.2 gather_fusion.1
  92.7 1.9 gather_fusion.2
  96.6 0.8 compare_and_fusion.11
  97.5 2.2 gather_fusion.1
  99.8 1.9 gather_fusion.2
  103.6 0.8 compare_and_fusion.11
  104.5 2.2 gather_fusion.1
  106.8 1.9 gather_fusion.2
  110.6 0.8 compare_and_fusion.11
  111.5 2.2 gather_fusion.1
  113.8 1.9 gather_fusion.2
  117.6 0.8 compare_and_fusion.11
  118.6 2.2 gather_fusion.1
  120.8 1.9 gather_fusion.2
  124.7 0.8 compare_and_fusion.11
  125.6 2.2 gather_fusion.1
  127.8 1.9 gather_fusion.2
  131.7 0.8 compare_and_fusion.11
  132.6 2.2 gather_fusion.1
  134.8 1.9 gather_fusion.2
  138.7 0.8 compare_and_fusion.11
  139.6 2.2 gather_fusion.1
  141.8 1.9 gather_fusion.2
  145.7 0.8 compare_and_fusion.11
  146.6 2.2 gather_fusion.1
  148.9 1.9 gather_fusion.2
  153.4 299.2 %reduce-scatter.3.cloned.1.call-done = f32[4,8,128]{2,1,0:T(8,128)} async-done(((f32[4,128,128]{2,1,0:T(8,128)}), f32[4,8,128]{2,1,0:T(8,128)}) %reduce-scatter.3.cloned.1.call-update) | async-done | bytes 16400 | tf_op jit(solution)/shard_map/reduce_scatter | solution.py:62
  452.6 1.5 fusion.54
  454.1 79.9 %all-reduce = (f32[]{:T(128)}, f32[]{:T(128)}) all-reduce(f32[]{:T(128)} %get-tuple-element.195, f32[]{:T(128)} %get-tuple-element.194), channel_id=1, replica_groups=mesh['term'=16,'sector'=16] {'term','sector'}, use_global_device_ids=true, to_apply=%region_4.7 | all-reduce | flops 2 | bytes 16 | tf_op jit(solution)/shard_map/psum | solution.py:106
  535.9 73.4 %psum.23 = f32[]{:T(128)} all-reduce(f32[]{:T(128)} %multiply_reduce_fusion), channel_id=1, replica_groups=mesh['term'=16,'sector'=16] {'term','sector'}, use_global_device_ids=true, to_apply=%region_8.11 | all-reduce | flops 1 | bytes 8 | tf_op jit(solution)/shard_map/psum | solution.py:111
  610.1 33.5 %all_gather.14 = bf16[4,128,128]{2,1,0:T(8,128)(2,1)} all-gather(bf16[4,8,128]{2,1,0:T(8,128)(2,1)S(1)} %multiply_convert_fusion), channel_id=1, replica_groups=mesh['term'=16,'sector'=16] {'term'}, dimensions={1}, use_global_device_ids=true | all-gather | bytes 139264 | tf_op jit(solution)/shard_map/all_gather | solution.py:15
  643.6 40.5 %all-gather.5.cloned.1.call-done = bf16[64,128,128]{2,1,0:T(8,128)(2,1)} async-done(((bf16[4,128,128]{2,1,0:T(8,128)(2,1)}), bf16[64,128,128]{2,1,0:T(8,128)(2,1)}) %all-gather.5.cloned.1.call-update) | async-done | bytes 2097168 | tf_op jit(solution)/shard_map/all_gather | solution.py:16
  684.2 63.2 %while.23 = (s32[]{:T(128)}, f32[4,128,128]{2,0,1:T(4,128)S(1)}, s32[]{:T(128)}, s32[384]{0:T(512)S(1)}, s32[]{:T(128)}, /*index=5*/s32[384]{0:T(512)S(1)}, bf16...) while((s32[]{:T(128)}, f32[4,128,128]{2,0,1:T(4,128)S(1)}, ...), condition=%wide.region_10.13_spmd.clone, body=%wide.region_9.12_spmd.clone.sunk | while | flops 137432528 | bytes 10499403 | solution.py:58
  685.2 2.2 gather_fusion.4
  687.5 1.9 gather_fusion.5
  691.3 0.8 compare_and_fusion.13
  692.2 2.2 gather_fusion.4
  694.5 1.9 gather_fusion.5
  699.3 2.2 gather_fusion.4
  701.5 1.9 gather_fusion.5
  705.4 0.8 compare_and_fusion.13
  706.3 2.2 gather_fusion.4
  708.5 1.9 gather_fusion.5
  712.4 0.8 compare_and_fusion.13
  713.3 2.2 gather_fusion.4
  715.5 1.9 gather_fusion.5
  719.4 0.8 compare_and_fusion.13
  720.3 2.2 gather_fusion.4
  722.6 1.9 gather_fusion.5
  726.4 0.8 compare_and_fusion.13
  727.3 2.2 gather_fusion.4
  729.6 1.9 gather_fusion.5
  733.4 0.8 compare_and_fusion.13
  734.3 2.2 gather_fusion.4
  736.6 1.9 gather_fusion.5
  740.4 0.8 compare_and_fusion.13
  741.4 2.2 gather_fusion.4
  743.6 1.9 gather_fusion.5
  748.1 299.3 %reduce-scatter.5.cloned.1.call-done = f32[4,8,128]{2,1,0:T(8,128)} async-done(((f32[4,128,128]{2,1,0:T(8,128)}), f32[4,8,128]{2,1,0:T(8,128)}) %reduce-scatter.5.cloned.1.call-update) | async-done | bytes 16400 | tf_op jit(solution)/shard_map/reduce_scatter | solution.py:62
  1047.4 1.4 and_select_fusion
  (211 shorter events, 45.1 us)
Async XLA Ops:
  7.2 82.2 %all-gather.3.cloned.1.call-start = ((), (), s32[]{:S(2)}) async-start(), calls=%async_computation.2 | async-start | bytes 2228224 | tf_op jit(solution)/shard_map/all_gather | solution.py:16
  49.9 402.7 %reduce-scatter.3.cloned.1.call-start = ((), (), s32[]{:S(2)}) async-start(), calls=%async_computation.3 | async-start | bytes 278528 | tf_op jit(solution)/shard_map/reduce_scatter | solution.py:62
  89.4 363.2 %copy-start.3 = (bf16[4,8,128]{2,1,0:T(8,128)(2,1)S(1)}, bf16[4,8,128]{2,1,0:T(8,128)(2,1)}, u32[]{:S(2)}) copy-start(bf16[4,8,128]{2,1,0:T(8,128)(2,1)} %param.18) | copy-start | bytes 24580
  89.5 363.2 %copy-start.4 = (f32[4,8,128]{2,1,0:T(8,128)S(1)}, f32[4,8,128]{2,1,0:T(8,128)}, u32[]{:S(2)}) copy-start(f32[4,8,128]{2,1,0:T(8,128)} %param.19) | copy-start | bytes 49156
  89.5 5.1 copy-start
  96.5 5.1 copy-start
  103.5 5.1 copy-start
  110.5 5.1 copy-start
  117.5 5.1 copy-start
  124.6 5.1 copy-start
  131.6 5.1 copy-start
  138.6 5.1 copy-start
  145.6 5.1 copy-start
  153.4 530.8 %all-gather.5.cloned.1.call-start = ((), (), s32[]{:S(2)}) async-start(), calls=%async_computation.4 | async-start | bytes 2228224 | tf_op jit(solution)/shard_map/all_gather | solution.py:16
  454.1 230.1 %copy-start.2 = (f32[4,8,128]{2,1,0:T(8,128)}, f32[4,8,128]{2,1,0:T(8,128)S(1)}, u32[]{:S(2)}) copy-start(f32[4,8,128]{2,1,0:T(8,128)S(1)} %get-tuple-element.254) | copy-start | bytes 49156
  643.6 403.8 %reduce-scatter.5.cloned.1.call-start = ((), (), s32[]{:S(2)}) async-start(), calls=%async_computation.5 | async-start | bytes 278528 | tf_op jit(solution)/shard_map/reduce_scatter | solution.py:62
  684.2 5.1 copy-start.1
  691.2 5.1 copy-start.1
  698.3 5.1 copy-start.1
  705.3 5.1 copy-start.1
  712.3 5.1 copy-start.1
  719.3 5.1 copy-start.1
  726.3 5.1 copy-start.1
  733.3 5.1 copy-start.1
  740.4 5.1 copy-start.1
Sparse Core Ops, SparseCore 0:
  50.0 39.3 all-gather.2
  153.5 299.0 reduce-scatter.2
  643.7 40.4 all-gather.4
  748.2 299.0 reduce-scatter.4
where the time goes:
time: 1060 us
  waiting for transfers between devices  675 us (64%)
  blocking collectives  228 us (22%)
  local copies, waits for them, and re-layouts  89.4 us (8%)
  other arithmetic  23.5 us (2%)
  matrix products  21.7 us (2%)
  between operations  16.4 us (2%)
    reduce_scatter x2, waiting for transfers between devices, reduce_split(): lax.psum_scatter(partial_sums, 'term', scatter_dimension=1, tiled=True)  598 us
    psum x1, blocking collectives, body(): lax.psum((jnp.sum(start_float * sigma_one), jnp.sum(start_float * start_f...  79.9 us
    all_gather x2, waiting for transfers between devices, collect(): return lax.all_gather(whole_rows, 'sector', axis=0, tiled=True)  76.6 us
    all_gather x2, blocking collectives, collect(): whole_rows = lax.all_gather(vector_here, 'term', axis=1, tiled=True)  74.4 us
    psum x1, blocking collectives, body(): resid_total = lax.psum(jnp.sum(residual * residual), ('term', 'sector'))  73.4 us
    gather x18, local copies, waits for them, and re-layouts, accumulate(): moved = jnp.take(full_vector, source_part, axis=0)  40.3 us
    gather x18, local copies, waits for them, and re-layouts, accumulate(): left_ops = jnp.take(left_tiles, left_part, axis=0)  33.7 us
  transfers between devices with their start and end apart: 4, of which 4 were waited for; matrix products, arithmetic and copies ran while one was open for 0% of the time, Pallas kernels for 0%

commit v1 on v0

v1 whole, which is shorter than its diff:
```python
import functools

import jax
import jax.numpy as jnp
from jax import lax
from jax.experimental import pallas as pl
from jax.experimental.pallas import tpu as pltpu
from jax.sharding import PartitionSpec as P

F32 = jnp.float32
BF16 = jnp.bfloat16
I32 = jnp.int32
MESH = pl.DeviceIdType.MESH

TILE = 128
PAIRS = 384
ENV = 32
BLK = 4
ROWS = 8
NX, NY, NZ, NCORE = 4, 4, 8, 2
N_TERM, N_SECTOR = 16, 16
NBLK = N_SECTOR * BLK
GROUPS = ENV * BLK
UNROLL = 32
N_SEND = 160
NT = (((1,), (1,)), ((), ()))


def dot(a, b):
    return jnp.dot(a, b, preferred_element_type=F32)


def as_bf16(flags):
    return flags.astype(F32).astype(BF16)


def schedule(source, target, left, right, count, steps_ref, last_ref):
    slot = lax.broadcasted_iota(I32, (1, PAIRS), 1)
    live = slot < count
    key = jnp.where(live, left * BLK + target, GROUPS)
    member = lax.broadcasted_iota(I32, (GROUPS, PAIRS), 0) == key
    member_f = member.astype(F32)
    member_b = member_f.astype(BF16)
    earlier = as_bf16(
        lax.broadcasted_iota(I32, (PAIRS, PAIRS), 0) < lax.broadcasted_iota(I32, (PAIRS, PAIRS), 1)
    )
    rank = jnp.sum(member_f * dot(member_b, earlier), axis=0, keepdims=True)
    row_g = lax.broadcasted_iota(I32, (GROUPS, GROUPS), 0)
    col_g = lax.broadcasted_iota(I32, (GROUPS, GROUPS), 1)
    size = jnp.broadcast_to(jnp.sum(member_f, axis=1, keepdims=True), (GROUPS, GROUPS))
    high = jnp.floor(size * (1.0 / 16.0))
    low = size - 16.0 * high
    below = as_bf16(col_g < row_g)
    begin = 16.0 * dot(below, high.astype(BF16)) + dot(below, low.astype(BF16))
    begin_of = jnp.sum(member_f * begin[:, :1], axis=0, keepdims=True)
    place = jnp.where(live, (rank + begin_of).astype(I32), -1)
    sent = as_bf16(lax.broadcasted_iota(I32, (PAIRS, PAIRS), 0) == place)
    line = lax.broadcasted_iota(I32, (8, PAIRS), 0)
    table = jnp.where(line == 0, source, jnp.where(line == 1, right, jnp.where(line == 2, key, 0)))
    moved = lax.dot_general(table.astype(F32).astype(BF16), sent, NT, preferred_element_type=F32)
    again = (moved == pltpu.roll(moved, 1, 1)) & (lax.broadcasted_iota(I32, (8, PAIRS), 1) > 0)
    top = jnp.where(line == 0, NBLK - 1, jnp.where(line == 1, ENV - 1, 1))
    steps_ref[...] = jnp.clip(jnp.where(line == 2, again.astype(I32), moved.astype(I32)), 0, top)
    size = lax.dot_general(jnp.ones((8, PAIRS), BF16), member_b, NT, preferred_element_type=F32)
    high = jnp.floor(size * (1.0 / 16.0))
    low = size - 16.0 * high
    above = as_bf16(row_g < col_g)
    begin = 16.0 * dot(high.astype(BF16), above) + dot(low.astype(BF16), above)
    ends = (begin + size).astype(I32) - 1
    last_ref[...] = jnp.where(size > 0.5, jnp.clip(ends, 0, PAIRS - 1), PAIRS)


def contract(steps, last, vector, lefts, rights, prefix, total):
    def step_body(turn, running):
        for u in range(UNROLL):
            k = turn * UNROLL + u
            keep = steps[2, k].astype(F32)
            running = running * keep + dot(vector[steps[0, k]], rights[steps[1, k]])
            prefix[k] = running.astype(BF16)
        return running

    lax.fori_loop(0, PAIRS // UNROLL, step_body, jnp.zeros((TILE, TILE), F32))
    for half in range(2):

        def left_body(turn, running):
            for u in range(4):
                l = (turn * 4 + u) * 2
                tiles = jnp.concatenate([lefts[l], lefts[l + 1]], axis=1)
                sums = [
                    jnp.concatenate(
                        [prefix[last[0, (l + dl) * BLK + half * 2 + db]] for db in range(2)], axis=1
                    )
                    for dl in range(2)
                ]
                running = running + dot(tiles, jnp.concatenate(sums, axis=0))
            return running

        both = lax.fori_loop(0, ENV // 8, left_body, jnp.zeros((TILE, 2 * TILE), F32))
        total[half * 2] = both[:, :TILE]
        total[half * 2 + 1] = both[:, TILE:]


def device_of(x, y, z, core):
    return (z * 2 + lax.div(y, 2), x * 4 + lax.rem(y, 2) * 2 + core)


class Links:
    def __init__(self, send_sem, recv_sem):
        self.send_sem, self.recv_sem = send_sem, recv_sem
        self.used = 0
        self.started = []

    def slot(self):
        self.used += 1
        return self.used - 1

    def copy(self, ref, slot, device, dst=None):
        return pltpu.make_async_remote_copy(
            src_ref=ref,
            dst_ref=ref if dst is None else dst,
            send_sem=self.send_sem.at[slot],
            recv_sem=self.recv_sem.at[slot],
            device_id=device,
            device_id_type=MESH,
        )

    def send(self, ref, slot, device, dst=None):
        copy = self.copy(ref, slot, device, dst)
        copy.start()
        self.started.append(copy)

    def arrived(self, ref, slot, device):
        self.copy(ref, slot, device).wait_recv()

    def drain(self):
        for copy in self.started:
            copy.wait_send()
        self.started = []


def gather(links, raw, at, meanwhile):
    x, y, z, core = at
    mate = device_of(x, y, z, 1 - core)

    def along(axis, step):
        if axis == "x":
            return device_of(lax.rem(x + step + NX, NX), y, z, core)
        return device_of(x, lax.rem(y + step + NY, NY), z, core)

    slots = [links.slot() for _ in range(1, NZ)]
    for d in (4, 3, 5, 2, 6, 1, 7):
        to = device_of(x, y, lax.rem(z + d, NZ), core)
        links.send(raw.at[:, core, x, y, z], slots[d - 1], to)
    meanwhile()
    for d in range(1, NZ):
        begin = lax.rem(z - d + NZ, NZ)
        links.arrived(raw.at[:, core, x, y, begin], slots[d - 1], device_of(x, y, begin, core))

    handed = []

    def hand(pick):
        slot = links.slot()
        links.send(pick(core), slot, mate)
        handed.append((pick, slot))

    class Ring:
        def __init__(self, axis, pick, parts):
            self.axis, self.pick, self.parts = axis, pick, parts
            self.here = x if axis == "x" else y
            self.slots = [links.slot() for _ in range(4)]

        def index(self, step):
            return lax.rem(self.here + step + 4, 4)

        def start(self):
            links.send(self.pick(core, self.here), self.slots[0], along(self.axis, 1))
            links.send(self.pick(core, self.here), self.slots[1], along(self.axis, -1))

        def relay(self, side):
            piece = self.index(side)
            back = 0 if side == -1 else 1
            links.arrived(self.pick(core, piece), self.slots[back], along(self.axis, side))
            half = self.parts(self.pick(core, piece), back)
            links.send(half, self.slots[2 + back], along(self.axis, -side))
            hand(lambda c: self.pick(c, piece))

        def finish(self):
            piece = self.index(2)
            for back, side in ((0, -1), (1, 1)):
                half = self.parts(self.pick(core, piece), back)
                links.arrived(half, self.slots[2 + back], along(self.axis, side))
            hand(lambda c: self.pick(c, piece))

    near = pl.ds(0, 4), pl.ds(4, 4)
    pair = pl.ds(0, 2), pl.ds(2, 2)
    hand(lambda c: raw.at[:, c, x, y])
    first = Ring("y", lambda c, i: raw.at[0, c, x, i], lambda ref, k: ref.at[near[k]])
    second = Ring("x", lambda c, i: raw.at[1, c, i, y], lambda ref, k: ref.at[near[k]])
    wide_first = Ring("x", lambda c, i: raw.at[0, c, i], lambda ref, k: ref.at[pair[k]])
    wide_second = Ring("y", lambda c, i: raw.at[1, c, :, i], lambda ref, k: ref.at[pair[k]])
    first.start()
    second.start()
    for side in (-1, 1):
        first.relay(side)
        second.relay(side)
    first.finish()
    wide_first.start()
    second.finish()
    wide_second.start()
    for side in (-1, 1):
        wide_first.relay(side)
        wide_second.relay(side)
    wide_first.finish()
    wide_second.finish()
    for pick, slot in handed:
        links.arrived(pick(1 - core), slot, mate)
    links.drain()


def settle(raw, vector):
    def body(turn, squares):
        h = lax.div(turn, 8)
        core = lax.rem(lax.div(turn, 4), 2)
        x = lax.rem(turn, 4)
        for y_lo in range(2):
            halves = [
                raw[h, core, x, y_hi * 2 + y_lo].astype(F32).reshape(NZ, 2, ROWS, TILE) for y_hi in range(2)
            ]
            for k in range(2):
                tile = jnp.stack([halves[0][:, k], halves[1][:, k]], axis=1)
                squares = squares + jnp.sum((tile * tile).reshape(2 * NZ, ROWS, TILE), axis=0)
                block = (x * 4 + y_lo * 2 + core) * BLK + h * 2 + k
                vector[block] = tile.reshape(TILE, TILE).astype(BF16)
        return squares

    return lax.fori_loop(0, 2 * NCORE * NX, body, jnp.zeros((ROWS, TILE), F32))


def spread(links, total, out, back, me, at_term):
    for h in range(2):
        rows = [total[h * 2 + k].reshape(N_TERM, ROWS, TILE) for k in range(2)]
        both = jnp.stack(rows, axis=1).reshape(N_TERM, 2 * ROWS, TILE).astype(BF16)
        out[:, h] = both
    slots = [links.slot() for _ in range(1, N_TERM)]
    for d in range(1, N_TERM):
        peer = lax.rem(me + d, N_TERM)
        links.send(out.at[peer], slots[d - 1], at_term(peer), back.at[d])
    return slots


def merge(links, slots, out, back, me, at_term):
    acc = out[me].astype(F32)
    for d in range(1, N_TERM):
        peer = lax.rem(me - d + N_TERM, N_TERM)
        links.arrived(back.at[d], slots[d - 1], at_term(peer))
        acc = acc + back[d].astype(F32)
    return acc.reshape(BLK, ROWS, TILE)


def everyone(links, mine, back, here, n, at):
    slots = [links.slot() for _ in range(1, n)]
    for d in range(1, n):
        links.send(mine, slots[d - 1], at(lax.rem(here + d, n)), back.at[d])

    def wait():
        acc = mine[...]
        for d in range(1, n):
            links.arrived(back.at[d], slots[d - 1], at(lax.rem(here - d + n, n)))
            acc = acc + back[d]
        return acc

    return wait


def kernel(
    psi,
    diag,
    shape,
    env_left,
    env_right,
    source,
    target,
    left,
    right,
    count,
    sigma_one,
    sigma_two,
    raw_one,
    raw_two,
    vector,
    lefts,
    rights,
    prefix,
    total,
    out_one,
    out_two,
    back_one,
    back_two,
    part,
    part_sector,
    part_term,
    steps_v,
    last_v,
    steps_s,
    last_s,
    local_sem,
    send_sem,
    recv_sem,
):
    term, sector = lax.axis_index("term"), lax.axis_index("sector")
    z, y_hi = lax.div(term, 2), lax.rem(term, 2)
    x, y_lo, core = lax.div(sector, 4), lax.rem(lax.div(sector, 2), 2), lax.rem(sector, 2)
    y = y_hi * 2 + y_lo
    at = (x, y, z, core)

    def at_term(t):
        return (t, sector)

    def at_sector(s):
        return (term, s)

    barrier = pltpu.get_barrier_semaphore()
    greeted = [at_term(lax.rem(term + d, N_TERM)) for d in range(1, N_TERM)]
    greeted += [at_sector(lax.rem(sector + d, N_SECTOR)) for d in range(1, N_SECTOR)]
    greeted += [(z * 2 + 1 - y_hi, x * 4 + (1 - y_lo) * 2 + core)]
    for device in greeted:
        pl.semaphore_signal(barrier, inc=1, device_id=device, device_id_type=MESH)

    fetch_left = pltpu.make_async_copy(env_left.at[0, 0], lefts, local_sem.at[0])
    fetch_right = pltpu.make_async_copy(env_right.at[0, 0], rights, local_sem.at[1])
    fetch_left.start()
    fetch_right.start()

    row = lax.broadcasted_iota(I32, (ROWS, TILE), 0) + term * ROWS
    col = lax.broadcasted_iota(I32, (ROWS, TILE), 1)
    inside = [(row < shape[b, 0]) & (col < shape[b, 1]) for b in range(BLK)]
    start = [jnp.where(inside[b], psi[b].astype(F32), 0.0) for b in range(BLK)]
    for h in range(2):
        raw_one[h, core, x, y, z] = jnp.concatenate(start[h * 2 : h * 2 + 2], axis=0).astype(BF16)
    prefix[PAIRS] = jnp.zeros((TILE, TILE), BF16)

    links = Links(send_sem, recv_sem)
    pl.semaphore_wait(barrier, len(greeted))

    def plan():
        schedule(source[0], target[0], left[0], right[0], count[0, 0], steps_v, last_v)
        copies = [
            pltpu.make_async_copy(steps_v, steps_s, local_sem.at[2]),
            pltpu.make_async_copy(last_v, last_s, local_sem.at[3]),
        ]
        for copy in copies:
            copy.start()
        for copy in copies:
            copy.wait()

    gather(links, raw_one, at, plan)
    start_squares = jnp.sum(settle(raw_one, vector), keepdims=True)
    fetch_left.wait()
    fetch_right.wait()
    contract(steps_s, last_s, vector, lefts, rights, prefix, total)

    overlap = jnp.zeros((ROWS, TILE), F32)
    for b in range(BLK):
        overlap = overlap + start[b] * start[b] * diag[b]
        both = vector[sector * BLK + b].astype(F32) * total[b]
        overlap = overlap + jnp.sum(both.reshape(TILE // ROWS, ROWS, TILE), axis=0)
    part[0] = overlap
    sector_sum = everyone(links, part.at[0], part_sector, sector, N_SECTOR, at_sector)
    slots = spread(links, total, out_one, back_one, term, at_term)
    part[1] = sector_sum()
    term_sum = everyone(links, part.at[1], part_term, term, N_TERM, at_term)
    coupled = merge(links, slots, out_one, back_one, term, at_term)
    sigma = [jnp.where(inside[b], diag[b] * start[b] + coupled[b], 0.0) for b in range(BLK)]
    for b in range(BLK):
        sigma_one[b] = sigma[b]
    rayleigh = jnp.sum(term_sum(), keepdims=True) / start_squares
    residual = [sigma[b] - rayleigh * start[b] for b in range(BLK)]
    for h in range(2):
        raw_two[h, core, x, y, z] = jnp.concatenate(residual[h * 2 : h * 2 + 2], axis=0).astype(BF16)
    links.drain()

    gather(links, raw_two, at, lambda: None)
    squares = jnp.sum(settle(raw_two, vector), keepdims=True)
    scale = lax.rsqrt(squares / float(NBLK * TILE * TILE) + 1e-06)
    contract(steps_s, last_s, vector, lefts, rights, prefix, total)
    slots = spread(links, total, out_two, back_two, term, at_term)
    coupled = merge(links, slots, out_two, back_two, term, at_term)
    for b in range(BLK):
        second = residual[b].astype(BF16).astype(F32)
        sigma_two[b] = jnp.where(inside[b], (diag[b] * second + coupled[b]) * scale, 0.0)
    links.drain()


def body(*args):
    vmem = pl.BlockSpec(memory_space=pltpu.VMEM)
    smem = pl.BlockSpec(memory_space=pltpu.SMEM)
    hbm = pl.BlockSpec(memory_space=pl.ANY)
    out = jax.ShapeDtypeStruct((BLK, ROWS, TILE), F32)
    raw = pltpu.VMEM((2, NCORE, NX, NY, NZ, 2 * ROWS, TILE), BF16)
    rows = pltpu.VMEM((N_TERM, 2, 2 * ROWS, TILE), BF16)
    return pl.pallas_call(
        kernel,
        out_shape=(out, out),
        in_specs=[vmem, vmem, smem, hbm, hbm, vmem, vmem, vmem, vmem, smem],
        out_specs=(vmem, vmem),
        scratch_shapes=[
            raw,
            raw,
            pltpu.VMEM((NBLK, TILE, TILE), BF16),
            pltpu.VMEM((ENV, TILE, TILE), BF16),
            pltpu.VMEM((ENV, TILE, TILE), BF16),
            pltpu.VMEM((PAIRS + 1, TILE, TILE), BF16),
            pltpu.VMEM((BLK, TILE, TILE), F32),
            rows,
            rows,
            rows,
            rows,
            pltpu.VMEM((2, ROWS, TILE), F32),
            pltpu.VMEM((N_SECTOR, ROWS, TILE), F32),
            pltpu.VMEM((N_TERM, ROWS, TILE), F32),
            pltpu.VMEM((8, PAIRS), I32),
            pltpu.VMEM((8, TILE), I32),
            pltpu.SMEM((8, PAIRS), I32),
            pltpu.SMEM((8, TILE), I32),
            pltpu.SemaphoreType.DMA((4,)),
            pltpu.SemaphoreType.DMA((N_SEND,)),
            pltpu.SemaphoreType.DMA((N_SEND,)),
        ],
        compiler_params=pltpu.CompilerParams(
            collective_id=0, has_side_effects=True, vmem_limit_bytes=48 * 2**20
        ),
        name="two_products",
    )(*args)


def solution(mesh):
    placed = (
        P("sector", "term", None),
        P("sector", "term", None),
        P("sector", None),
        P("term", "sector", None, None, None),
        P("term", "sector", None, None, None),
        P("term", "sector", None),
        P("term", "sector", None),
        P("term", "sector", None),
        P("term", "sector", None),
        P("term", "sector"),
    )
    return jax.shard_map(
        body,
        mesh=mesh,
        in_specs=placed,
        out_specs=(P("sector", "term", None), P("sector", "term", None)),
        check_vma=False,
    )
```

time: 1060 us -> 100 us (0.09)
  waiting for transfers between devices: 675 us -> 0 us
  blocking collectives: 228 us -> 0 us
  Pallas kernels: 0 us -> 92.2 us
  local copies, waits for them, and re-layouts: 89.4 us -> 6.54 us
  other arithmetic: 23.5 us -> 0 us
  matrix products: 21.7 us -> 0 us
  between operations: 16.4 us -> 1.34 us
    reduce_scatter x2 -> x0, waiting for transfers between devices: 598 us -> none  [reduce_split(): lax.psum_scatter(partial_sums, 'term', scatter_dimension=1, tiled=True)]
    psum x2 -> x0, blocking collectives: 153 us -> none  [the longest x1 79.9 us: body(): lax.psum((jnp.sum(start_float * sigma_one), jnp.sum(start_float * start_f...]
    pallas_call x0 -> x1, Pallas kernels: none -> 92.2 us  [body(): pl.pallas_call(kernel, out_shape=(out, out), in_specs=[vmem, vmem, smem,...]
    gather x54 -> x0, local copies, waits for them, and re-layouts: 85.7 us -> none  [the longest x18 40.3 us: accumulate(): moved = jnp.take(full_vector, source_part, axis=0)]
    all_gather x2 -> x0, waiting for transfers between devices: 76.6 us -> none  [collect(): return lax.all_gather(whole_rows, 'sector', axis=0, tiled=True)]
    all_gather x2 -> x0, blocking collectives: 74.4 us -> none  [collect(): whole_rows = lax.all_gather(vector_here, 'term', axis=1, tiled=True)]
    dot_general x36 -> x0, matrix products: 21.7 us -> none  [the longest x18 12.5 us: accumulate(): return running + jnp.einsum('pb,pxy->bxy', onehot, product)]
    and x36 -> x0, other arithmetic: 15.8 us -> none  [the longest x18 14.4 us: accumulate(): left_ops = jnp.take(left_tiles, left_part, axis=0)]
  transfers between devices with their start and end apart: 4 -> 0, of which waited for: 4 -> 0; matrix products, arithmetic and copies ran while one was open for 0% -> 0% of each run, Pallas kernels for 0% -> 0%
where the time goes in v1:
time: 100 us
  Pallas kernels  92.2 us (92%)
  local copies, waits for them, and re-layouts  6.54 us (7%)
  between operations  1.34 us (1%)
    pallas_call x1, Pallas kernels, body(): pl.pallas_call(kernel, out_shape=(out, out), in_specs=[vmem, vmem, smem,...  92.2 us
    unnamed x19, local copies, waits for them, and re-layouts  6.54 us

profile of v1, /device:TPU:1, one launch (start us, length us, event | category | flops | bytes accessed | tf_op | source)
XLA Modules:
  0.0 100.1 jit_solution(3629856617778343443)
XLA Ops:
  0.6 0.0 copy-start.6
  1.3 0.0 copy-start.4
  1.3 0.0 copy-start.5
  1.3 0.8 copy.12.shape
  2.1 0.0 copy-done.6
  2.1 0.0 copy-done.4
  2.1 0.0 copy-done.5
  2.1 0.0 copy-start
  2.1 1.2 %copy-done = bf16[1,1,32,128,128]{4,3,2,1,0:T(8,128)(2,1)S(1)} copy-done((bf16[1,1,32,128,128]{4,3,2,1,0:T(8,128)(2,1)S(1)}, bf16[1,1,32,128,128]{4,3,2,1,0:T(8,128)(2,1)}, u32[]{:S(2)}) %copy-start) | copy-done | bytes 1048600
  3.3 0.0 copy-start.1
  3.3 1.2 %copy-done.1 = bf16[1,1,32,128,128]{4,3,2,1,0:T(8,128)(2,1)S(1)} copy-done((bf16[1,1,32,128,128]{4,3,2,1,0:T(8,128)(2,1)S(1)}, bf16[1,1,32,128,128]{4,3,2,1,0:T(8,128)(2,1)}, u32[]{:S(2)}) %copy-start.1) | copy-done | bytes 1048600
  4.6 0.0 copy-start.2
  4.6 0.7 copy-done.2
  5.3 0.0 copy-start.3
  5.3 0.7 copy-done.3
  6.0 0.0 copy-start.7
  6.0 0.7 copy-done.7
  6.7 92.2 %two_products.1 = (f32[4,8,128]{2,1,0:T(8,128)S(1)}, f32[4,8,128]{2,1,0:T(8,128)S(1)}) custom-call(bf16[4,8,128]{2,1,0:T(8,128)(2,1)S(1)} %copy-done.3, f32[4,8,128]{2,1,0:T(8,128)S(1)} %copy-done.2, s32[4,2]{1,0:T(4,128)S(1)} %copy.12.shape, bf16[1,1,32,128,128]{4,3,2,1,0:T(8,128)(2,1)S(1)} %copy-done, bf16[1,1,32,128,128]{4,3,2,1,0:T(8,128)(2,1)S(1)} %copy-done.1, ...), custom_call_target="tpu_custom_call" | custom-call | tf_op jit(solution)/shard_map/two_products/pallas_call | solution.py:401
  98.9 0.6 copy.16
  99.5 0.6 copy.17
Async XLA Ops:
  0.6 1.5 %copy-start.6 = (s32[1,1,384]{2,1,0:T(1,128)S(1)}, s32[1,1,384]{2,1,0:T(1,128)}, u32[]{:S(2)}) copy-start(s32[1,1,384]{2,1,0:T(1,128)} %left.1) | copy-start | bytes 4612
  1.3 0.8 copy-start.4
  1.3 0.8 copy-start.5
  2.1 1.2 %copy-start = (bf16[1,1,32,128,128]{4,3,2,1,0:T(8,128)(2,1)S(1)}, bf16[1,1,32,128,128]{4,3,2,1,0:T(8,128)(2,1)}, u32[]{:S(2)}) copy-start(bf16[1,1,32,128,128]{4,3,2,1,0:T(8,128)(2,1)} %env_left.1) | copy-start | bytes 3145732
  3.3 1.2 %copy-start.1 = (bf16[1,1,32,128,128]{4,3,2,1,0:T(8,128)(2,1)S(1)}, bf16[1,1,32,128,128]{4,3,2,1,0:T(8,128)(2,1)}, u32[]{:S(2)}) copy-start(bf16[1,1,32,128,128]{4,3,2,1,0:T(8,128)(2,1)} %env_right.1) | copy-start | bytes 3145732
  4.6 0.7 copy-start.2
  5.3 0.7 copy-start.3
  6.0 0.7 copy-start.7

commit v2 on v1

--- a/solution.py
+++ b/solution.py
@@ -22,7 +22,9 @@
 NBLK = N_SECTOR * BLK
 GROUPS = ENV * BLK
 UNROLL = 32
-N_SEND = 160
+N_SEND = 192
+OFFSETS = (0, 1, -1, 2, -2, 3, -3, 4)
+ZGROUPS = ((0, 3), (3, 7), (7, 8))
 NT = (((1,), (1,)), ((), ()))
 
 
@@ -75,7 +77,8 @@
         for u in range(UNROLL):
             k = turn * UNROLL + u
             keep = steps[2, k].astype(F32)
-            running = running * keep + dot(vector[steps[0, k]], rights[steps[1, k]])
+            tile = vector[steps[0, k]].reshape(TILE, TILE)
+            running = running * keep + dot(tile, rights[steps[1, k]])
             prefix[k] = running.astype(BF16)
         return running
 
@@ -138,102 +141,93 @@
         self.started = []
 
 
-def gather(links, raw, at, meanwhile):
+def gather(links, raw, vector, at, ready):
     x, y, z, core = at
     mate = device_of(x, y, z, 1 - core)
-
-    def along(axis, step):
-        if axis == "x":
-            return device_of(lax.rem(x + step + NX, NX), y, z, core)
-        return device_of(x, lax.rem(y + step + NY, NY), z, core)
-
-    slots = [links.slot() for _ in range(1, NZ)]
-    for d in (4, 3, 5, 2, 6, 1, 7):
-        to = device_of(x, y, lax.rem(z + d, NZ), core)
-        links.send(raw.at[:, core, x, y, z], slots[d - 1], to)
-    meanwhile()
-    for d in range(1, NZ):
-        begin = lax.rem(z - d + NZ, NZ)
-        links.arrived(raw.at[:, core, x, y, begin], slots[d - 1], device_of(x, y, begin, core))
-
-    handed = []
-
-    def hand(pick):
+    squares = jnp.zeros((ROWS, TILE), F32)
+
+    def wrap(i):
+        return lax.rem(i, 4)
+
+    def along_x(step):
+        return device_of(wrap(x + step), y, z, core)
+
+    def along_y(step):
+        return device_of(x, wrap(y + step), z, core)
+
+    def exchange(along, mine, theirs):
+        slots = [links.slot() for _ in range(1, 4)]
+        for d in (2, 1, 3):
+            links.send(mine, slots[d - 1], along(d))
+
+        def wait():
+            for d in (1, 3, 2):
+                links.arrived(theirs(4 - d), slots[d - 1], along(4 - d))
+
+        return wait
+
+    near, far, handed = [], [], []
+    for begin, end in ZGROUPS:
+        for k in range(begin, end):
+            ready(k)
+        g = pl.ds(begin, end - begin)
+        near.append(
+            (
+                exchange(along_y, raw.at[0, core, x, y, g], lambda d, g=g: raw.at[0, core, x, wrap(y + d), g]),
+                exchange(along_x, raw.at[1, core, x, y, g], lambda d, g=g: raw.at[1, core, wrap(x + d), y, g]),
+            )
+        )
+    for (begin, end), (wait_y, wait_x) in zip(ZGROUPS, near):
+        g = pl.ds(begin, end - begin)
+        wait_y()
+        wait_first = exchange(along_x, raw.at[0, core, x, :, g], lambda d, g=g: raw.at[0, core, wrap(x + d), :, g])
+        wait_x()
+        wait_second = exchange(along_y, raw.at[1, core, :, y, g], lambda d, g=g: raw.at[1, core, :, wrap(y + d), g])
+        far.append((wait_first, wait_second))
+    for (begin, end), waits in zip(ZGROUPS, far):
+        g = pl.ds(begin, end - begin)
+        for wait in waits:
+            wait()
         slot = links.slot()
-        links.send(pick(core), slot, mate)
-        handed.append((pick, slot))
-
-    class Ring:
-        def __init__(self, axis, pick, parts):
-            self.axis, self.pick, self.parts = axis, pick, parts
-            self.here = x if axis == "x" else y
-            self.slots = [links.slot() for _ in range(4)]
-
-        def index(self, step):
-            return lax.rem(self.here + step + 4, 4)
-
-        def start(self):
-            links.send(self.pick(core, self.here), self.slots[0], along(self.axis, 1))
-            links.send(self.pick(core, self.here), self.slots[1], along(self.axis, -1))
-
-        def relay(self, side):
-            piece = self.index(side)
-            back = 0 if side == -1 else 1
-            links.arrived(self.pick(core, piece), self.slots[back], along(self.axis, side))
-            half = self.parts(self.pick(core, piece), back)
-            links.send(half, self.slots[2 + back], along(self.axis, -side))
-            hand(lambda c: self.pick(c, piece))
-
-        def finish(self):
-            piece = self.index(2)
-            for back, side in ((0, -1), (1, 1)):
-                half = self.parts(self.pick(core, piece), back)
-                links.arrived(half, self.slots[2 + back], along(self.axis, side))
-            hand(lambda c: self.pick(c, piece))
-
-    near = pl.ds(0, 4), pl.ds(4, 4)
-    pair = pl.ds(0, 2), pl.ds(2, 2)
-    hand(lambda c: raw.at[:, c, x, y])
-    first = Ring("y", lambda c, i: raw.at[0, c, x, i], lambda ref, k: ref.at[near[k]])
-    second = Ring("x", lambda c, i: raw.at[1, c, i, y], lambda ref, k: ref.at[near[k]])
-    wide_first = Ring("x", lambda c, i: raw.at[0, c, i], lambda ref, k: ref.at[pair[k]])
-    wide_second = Ring("y", lambda c, i: raw.at[1, c, :, i], lambda ref, k: ref.at[pair[k]])
-    first.start()
-    second.start()
-    for side in (-1, 1):
-        first.relay(side)
-        second.relay(side)
-    first.finish()
-    wide_first.start()
-    second.finish()
-    wide_second.start()
-    for side in (-1, 1):
-        wide_first.relay(side)
-        wide_second.relay(side)
-    wide_first.finish()
-    wide_second.finish()
-    for pick, slot in handed:
-        links.arrived(pick(1 - core), slot, mate)
-    links.drain()
-
-
-def settle(raw, vector):
-    def body(turn, squares):
-        h = lax.div(turn, 8)
-        core = lax.rem(lax.div(turn, 4), 2)
-        x = lax.rem(turn, 4)
-        for y_lo in range(2):
-            halves = [
-                raw[h, core, x, y_hi * 2 + y_lo].astype(F32).reshape(NZ, 2, ROWS, TILE) for y_hi in range(2)
-            ]
-            for k in range(2):
-                tile = jnp.stack([halves[0][:, k], halves[1][:, k]], axis=1)
-                squares = squares + jnp.sum((tile * tile).reshape(2 * NZ, ROWS, TILE), axis=0)
-                block = (x * 4 + y_lo * 2 + core) * BLK + h * 2 + k
-                vector[block] = tile.reshape(TILE, TILE).astype(BF16)
+        links.send(raw.at[:, core, :, :, g], slot, mate)
+        handed.append(slot)
+        squares = settle(raw, vector, z, core, begin, end, squares)
+    for (begin, end), slot in zip(ZGROUPS, handed):
+        links.arrived(raw.at[:, 1 - core, :, :, pl.ds(begin, end - begin)], slot, mate)
+        squares = settle(raw, vector, z, 1 - core, begin, end, squares)
+    return squares
+
+
+def settle(raw, vector, z, core, begin, end, squares):
+    def body(x, squares):
+        for h in range(2):
+            for y_lo in range(2):
+                block = (x * 4 + y_lo * 2 + core) * BLK + h * 2
+                for k in range(begin, end):
+                    origin = lax.rem(z + (OFFSETS[k] + NZ), NZ)
+                    low = raw[h, core, x, y_lo, k].astype(F32)
+                    high = raw[h, core, x, y_lo + 2, k].astype(F32)
+                    squares = squares + (low[:ROWS] * low[:ROWS] + low[ROWS:] * low[ROWS:])
+                    squares = squares + (high[:ROWS] * high[:ROWS] + high[ROWS:] * high[ROWS:])
+                    vector[block, origin] = jnp.concatenate([low[:ROWS], high[:ROWS]], axis=0).astype(BF16)
+                    vector[block + 1, origin] = jnp.concatenate([low[ROWS:], high[ROWS:]], axis=0).astype(BF16)
         return squares
 
-    return lax.fori_loop(0, 2 * NCORE * NX, body, jnp.zeros((ROWS, TILE), F32))
+    return lax.fori_loop(0, NX, body, squares)
+
+
+def along_z(links, mine, place, at):
+    x, y, z, core = at
+    slots = [links.slot() for _ in OFFSETS]
+    for k in (7, 5, 6, 3, 4, 1, 2):
+        links.send(mine, slots[k], device_of(x, y, lax.rem(z - OFFSETS[k] + NZ, NZ), core), place(k))
+
+    def wait(k):
+        if k:
+            origin = lax.rem(z + (OFFSETS[k] + NZ), NZ)
+            links.arrived(place(k), slots[k], device_of(x, y, origin, core))
+
+    return wait
 
 
 def spread(links, total, out, back, me, at_term):
@@ -273,20 +267,27 @@
 
 
 def kernel(
-    psi,
-    diag,
+    psi_hbm,
+    diag_hbm,
     shape,
     env_left,
     env_right,
+    source_hbm,
+    target_hbm,
+    left_hbm,
+    right_hbm,
+    count,
+    sigma_one,
+    sigma_two,
+    psi,
+    diag_rows,
     source,
     target,
     left,
     right,
-    count,
-    sigma_one,
-    sigma_two,
     raw_one,
     raw_two,
+    rows_f32,
     vector,
     lefts,
     rights,
@@ -319,6 +320,24 @@
     def at_sector(s):
         return (term, s)
 
+    fetches = [
+        pltpu.make_async_copy(here, there, local_sem.at[i])
+        for i, (here, there) in enumerate(
+            (
+                (psi_hbm, psi),
+                (diag_hbm, diag_rows),
+                (source_hbm, source),
+                (target_hbm, target),
+                (left_hbm, left),
+                (right_hbm, right),
+                (env_left.at[0, 0], lefts),
+                (env_right.at[0, 0], rights),
+            )
+        )
+    ]
+    for fetch in fetches:
+        fetch.start()
+
     barrier = pltpu.get_barrier_semaphore()
     greeted = [at_term(lax.rem(term + d, N_TERM)) for d in range(1, N_TERM)]
     greeted += [at_sector(lax.rem(sector + d, N_SECTOR)) for d in range(1, N_SECTOR)]
@@ -326,44 +345,42 @@
     for device in greeted:
         pl.semaphore_signal(barrier, inc=1, device_id=device, device_id_type=MESH)
 
-    fetch_left = pltpu.make_async_copy(env_left.at[0, 0], lefts, local_sem.at[0])
-    fetch_right = pltpu.make_async_copy(env_right.at[0, 0], rights, local_sem.at[1])
-    fetch_left.start()
-    fetch_right.start()
-
     row = lax.broadcasted_iota(I32, (ROWS, TILE), 0) + term * ROWS
     col = lax.broadcasted_iota(I32, (ROWS, TILE), 1)
-    inside = [(row < shape[b, 0]) & (col < shape[b, 1]) for b in range(BLK)]
-    start = [jnp.where(inside[b], psi[b].astype(F32), 0.0) for b in range(BLK)]
+    inside = [(row < shape[0, b]) & (col < shape[1, b]) for b in range(BLK)]
+    prefix[PAIRS] = jnp.zeros((TILE, TILE), BF16)
+    for fetch in fetches[:2]:
+        fetch.wait()
+    diag = diag_rows[...].reshape(BLK, ROWS, TILE)
+    given = [psi[h].astype(F32).reshape(2, ROWS, TILE) for h in range(2)]
+    start = [jnp.where(inside[b], given[b // 2][b % 2], 0.0) for b in range(BLK)]
     for h in range(2):
-        raw_one[h, core, x, y, z] = jnp.concatenate(start[h * 2 : h * 2 + 2], axis=0).astype(BF16)
-    prefix[PAIRS] = jnp.zeros((TILE, TILE), BF16)
+        raw_one[h, core, x, y, 0] = jnp.concatenate(start[h * 2 : h * 2 + 2], axis=0).astype(BF16)
 
     links = Links(send_sem, recv_sem)
     pl.semaphore_wait(barrier, len(greeted))
-
-    def plan():
-        schedule(source[0], target[0], left[0], right[0], count[0, 0], steps_v, last_v)
-        copies = [
-            pltpu.make_async_copy(steps_v, steps_s, local_sem.at[2]),
-            pltpu.make_async_copy(last_v, last_s, local_sem.at[3]),
-        ]
-        for copy in copies:
-            copy.start()
-        for copy in copies:
-            copy.wait()
-
-    gather(links, raw_one, at, plan)
-    start_squares = jnp.sum(settle(raw_one, vector), keepdims=True)
-    fetch_left.wait()
-    fetch_right.wait()
+    arrived = along_z(links, raw_one.at[:, core, x, y, 0], lambda k: raw_one.at[:, core, x, y, k], at)
+
+    for fetch in fetches[2:6]:
+        fetch.wait()
+    schedule(source[0], target[0], left[0], right[0], count[0, 0], steps_v, last_v)
+    copies = [
+        pltpu.make_async_copy(steps_v, steps_s, local_sem.at[8]),
+        pltpu.make_async_copy(last_v, last_s, local_sem.at[9]),
+    ]
+    for copy in copies:
+        copy.start()
+
+    start_squares = jnp.sum(gather(links, raw_one, vector, at, arrived), keepdims=True)
+    for copy in copies + fetches[6:]:
+        copy.wait()
     contract(steps_s, last_s, vector, lefts, rights, prefix, total)
 
     overlap = jnp.zeros((ROWS, TILE), F32)
     for b in range(BLK):
         overlap = overlap + start[b] * start[b] * diag[b]
-        both = vector[sector * BLK + b].astype(F32) * total[b]
-        overlap = overlap + jnp.sum(both.reshape(TILE // ROWS, ROWS, TILE), axis=0)
+        tile = vector[sector * BLK + b].astype(F32).reshape(N_TERM, ROWS, TILE)
+        overlap = overlap + jnp.sum(tile * total[b].reshape(N_TERM, ROWS, TILE), axis=0)
     part[0] = overlap
     sector_sum = everyone(links, part.at[0], part_sector, sector, N_SECTOR, at_sector)
     slots = spread(links, total, out_one, back_one, term, at_term)
@@ -372,41 +389,54 @@
     coupled = merge(links, slots, out_one, back_one, term, at_term)
     sigma = [jnp.where(inside[b], diag[b] * start[b] + coupled[b], 0.0) for b in range(BLK)]
     for b in range(BLK):
+        rows_f32[0, b] = sigma[b]
+    arrived_f32 = along_z(links, rows_f32.at[0], lambda k: rows_f32.at[k], at)
+    for b in range(BLK):
         sigma_one[b] = sigma[b]
     rayleigh = jnp.sum(term_sum(), keepdims=True) / start_squares
-    residual = [sigma[b] - rayleigh * start[b] for b in range(BLK)]
-    for h in range(2):
-        raw_two[h, core, x, y, z] = jnp.concatenate(residual[h * 2 : h * 2 + 2], axis=0).astype(BF16)
-    links.drain()
-
-    gather(links, raw_two, at, lambda: None)
-    squares = jnp.sum(settle(raw_two, vector), keepdims=True)
+
+    def residual_here(k):
+        arrived_f32(k)
+        for h in range(2):
+            before = raw_one[h, core, x, y, k].astype(F32)
+            after = rows_f32[k, h * 2 : h * 2 + 2].reshape(2 * ROWS, TILE)
+            raw_two[h, core, x, y, k] = (after - rayleigh * before).astype(BF16)
+
+    squares = jnp.sum(gather(links, raw_two, vector, at, residual_here), keepdims=True)
     scale = lax.rsqrt(squares / float(NBLK * TILE * TILE) + 1e-06)
     contract(steps_s, last_s, vector, lefts, rights, prefix, total)
     slots = spread(links, total, out_two, back_two, term, at_term)
     coupled = merge(links, slots, out_two, back_two, term, at_term)
     for b in range(BLK):
-        second = residual[b].astype(BF16).astype(F32)
+        second = raw_two[b // 2, core, x, y, 0].astype(F32)[(b % 2) * ROWS : (b % 2 + 1) * ROWS]
         sigma_two[b] = jnp.where(inside[b], (diag[b] * second + coupled[b]) * scale, 0.0)
     links.drain()
 
 
-def body(*args):
+def body(psi, diag_energy, block_shape, *rest):
     vmem = pl.BlockSpec(memory_space=pltpu.VMEM)
     smem = pl.BlockSpec(memory_space=pltpu.SMEM)
-    hbm = pl.BlockSpec(memory_space=pl.ANY)
+    hbm = pl.BlockSpec(memory_space=pltpu.HBM)
     out = jax.ShapeDtypeStruct((BLK, ROWS, TILE), F32)
     raw = pltpu.VMEM((2, NCORE, NX, NY, NZ, 2 * ROWS, TILE), BF16)
     rows = pltpu.VMEM((N_TERM, 2, 2 * ROWS, TILE), BF16)
+    slots = pltpu.VMEM((1, 1, PAIRS), I32)
     return pl.pallas_call(
         kernel,
         out_shape=(out, out),
-        in_specs=[vmem, vmem, smem, hbm, hbm, vmem, vmem, vmem, vmem, smem],
+        in_specs=[hbm, hbm, smem, hbm, hbm, hbm, hbm, hbm, hbm, smem],
         out_specs=(vmem, vmem),
         scratch_shapes=[
+            pltpu.VMEM((2, 2 * ROWS, TILE), BF16),
+            pltpu.VMEM((BLK * ROWS, TILE), F32),
+            slots,
+            slots,
+            slots,
+            slots,
             raw,
             raw,
-            pltpu.VMEM((NBLK, TILE, TILE), BF16),
+            pltpu.VMEM((NZ, BLK, ROWS, TILE), F32),
+            pltpu.VMEM((NBLK, NZ, 2 * ROWS, TILE), BF16),
             pltpu.VMEM((ENV, TILE, TILE), BF16),
             pltpu.VMEM((ENV, TILE, TILE), BF16),
             pltpu.VMEM((PAIRS + 1, TILE, TILE), BF16),
@@ -422,15 +452,15 @@
             pltpu.VMEM((8, TILE), I32),
             pltpu.SMEM((8, PAIRS), I32),
             pltpu.SMEM((8, TILE), I32),
-            pltpu.SemaphoreType.DMA((4,)),
+            pltpu.SemaphoreType.DMA((10,)),
             pltpu.SemaphoreType.DMA((N_SEND,)),
             pltpu.SemaphoreType.DMA((N_SEND,)),
         ],
         compiler_params=pltpu.CompilerParams(
-            collective_id=0, has_side_effects=True, vmem_limit_bytes=48 * 2**20
+            collective_id=0, has_side_effects=True, vmem_limit_bytes=60 * 2**20
         ),
         name="two_products",
-    )(*args)
+    )(psi.reshape(2, 2 * ROWS, TILE), diag_energy.reshape(BLK * ROWS, TILE), block_shape.T, *rest)
 
 
 def solution(mesh):

time: 100 us -> 79.5 us (0.80)
  Pallas kernels: 92.2 us -> 76.1 us
  local copies, waits for them, and re-layouts: 6.54 us -> 1.94 us
    pallas_call x1, Pallas kernels: 92.2 us -> 76.1 us  [body(): pl.pallas_call(kernel, out_shape=(out, out), in_specs=[hbm, hbm, smem, hb...]
    unnamed x19 -> x4, local copies, waits for them, and re-layouts: 6.54 us -> 1.94 us
where the time goes in v2:
time: 79.5 us; the launch traced here: 79.4 us
  Pallas kernels  76.1 us (96%)
  local copies, waits for them, and re-layouts  1.94 us (2%)
  between operations  1.3 us (2%)
    pallas_call x1, Pallas kernels, body(): pl.pallas_call(kernel, out_shape=(out, out), in_specs=[hbm, hbm, smem, hb...  76.1 us
    unnamed x4, local copies, waits for them, and re-layouts  1.94 us

profile of v2, /device:TPU:1, one launch (start us, length us, event | category | flops | bytes accessed | tf_op | source)
XLA Modules:
  0.0 79.4 jit_solution(15415826382653822282)
XLA Ops:
  1.3 76.1 %two_products.1 = (f32[4,8,128]{2,1,0:T(8,128)}, f32[4,8,128]{2,1,0:T(8,128)}) custom-call(bf16[2,16,128]{2,1,0:T(8,128)(2,1)} %bitcast.4, f32[32,128]{1,0:T(8,128)} %bitcast.3, s32[2,4]{1,0:T(2,128)} %bitcast.5, bf16[1,1,32,128,128]{4,3,2,1,0:T(8,128)(2,1)} %env_left.1, bf16[1,1,32,128,128]{4,3,2,1,0:T(8,128)(2,1)} %env_right.1, s32[1,1,384]{2,1,0:T(1,128)} %source_hbm.1, ...), custom_call_target="tpu_custom_call" | custom-call | tf_op jit(solution)/shard_map/two_products/pallas_call | solution.py:424
  77.4 0.0 copy-start
  77.4 1.3 %copy.15 = f32[4,8,128]{2,1,0:T(8,128)} copy(f32[4,8,128]{2,1,0:T(8,128)} %get-tuple-element.4) | data formatting | bytes 32768
  78.7 0.0 copy-done
  78.7 0.6 copy.16
Async XLA Ops:
  77.4 1.3 %copy-start = (f32[4,8,128]{2,1,0:T(8,128)S(1)}, f32[4,8,128]{2,1,0:T(8,128)}, u32[]{:S(2)}) copy-start(f32[4,8,128]{2,1,0:T(8,128)} %get-tuple-element.5) | copy-start | bytes 49156

commit v3 on v2

--- a/solution.py
+++ b/solution.py
@@ -21,10 +21,20 @@
 N_TERM, N_SECTOR = 16, 16
 NBLK = N_SECTOR * BLK
 GROUPS = ENV * BLK
-UNROLL = 32
-N_SEND = 192
+UNROLL = 96
+N_SEND = 64
 OFFSETS = (0, 1, -1, 2, -2, 3, -3, 4)
-ZGROUPS = ((0, 3), (3, 7), (7, 8))
+ZGROUPS = ((0, 1), (1, 3), (3, 5), (5, 7), (7, 8))
+
+
+def order_of(*marks):
+    names = {"n": "near", "f": "far", "h": "hand", "t": "take"}
+    return tuple((names[mark[0]], int(mark[1:])) for mark in marks)
+
+
+ENDS = ("h0", "h1", "t0", "h2", "t1", "h3", "t2", "h4", "t3", "t4")
+ORDER_ONE = order_of("n0", "n1", "n2", "f0", "n3", "n4", "f1", "f2", "f3", "f4", *ENDS)
+ORDER_TWO = order_of("n0", "n1", "n2", "n3", "n4", "f0", "f1", "f2", "f3", "f4", *ENDS)
 NT = (((1,), (1,)), ((), ()))
 
 
@@ -84,23 +94,16 @@
 
     lax.fori_loop(0, PAIRS // UNROLL, step_body, jnp.zeros((TILE, TILE), F32))
     for half in range(2):
-
-        def left_body(turn, running):
-            for u in range(4):
-                l = (turn * 4 + u) * 2
-                tiles = jnp.concatenate([lefts[l], lefts[l + 1]], axis=1)
-                sums = [
-                    jnp.concatenate(
-                        [prefix[last[0, (l + dl) * BLK + half * 2 + db]] for db in range(2)], axis=1
-                    )
-                    for dl in range(2)
-                ]
-                running = running + dot(tiles, jnp.concatenate(sums, axis=0))
-            return running
-
-        both = lax.fori_loop(0, ENV // 8, left_body, jnp.zeros((TILE, 2 * TILE), F32))
-        total[half * 2] = both[:, :TILE]
-        total[half * 2 + 1] = both[:, TILE:]
+        running = jnp.zeros((TILE, 2 * TILE), F32)
+        for l in range(0, ENV, 2):
+            tiles = jnp.concatenate([lefts[l], lefts[l + 1]], axis=1)
+            sums = [
+                jnp.concatenate([prefix[last[0, (l + dl) * BLK + half * 2 + db]] for db in range(2)], axis=1)
+                for dl in range(2)
+            ]
+            running = running + dot(tiles, jnp.concatenate(sums, axis=0))
+        total[half * 2] = running[:, :TILE]
+        total[half * 2 + 1] = running[:, TILE:]
 
 
 def device_of(x, y, z, core):
@@ -108,13 +111,14 @@
 
 
 class Links:
-    def __init__(self, send_sem, recv_sem):
-        self.send_sem, self.recv_sem = send_sem, recv_sem
+    def __init__(self, send_sem, recv_sem, device):
+        self.send_sem, self.recv_sem, self.device = send_sem, recv_sem, device
         self.used = 0
-        self.started = []
-
-    def slot(self):
+        self.pending = []
+
+    def slot(self, whole):
         self.used += 1
+        self.pending.append((whole, self.used - 1))
         return self.used - 1
 
     def copy(self, ref, slot, device, dst=None):
@@ -128,20 +132,18 @@
         )
 
     def send(self, ref, slot, device, dst=None):
-        copy = self.copy(ref, slot, device, dst)
-        copy.start()
-        self.started.append(copy)
-
-    def arrived(self, ref, slot, device):
-        self.copy(ref, slot, device).wait_recv()
-
-    def drain(self):
-        for copy in self.started:
-            copy.wait_send()
-        self.started = []
-
-
-def gather(links, raw, vector, at, ready):
+        self.copy(ref, slot, device, dst).start()
+
+    def arrived(self, whole, slot):
+        self.copy(whole, slot, self.device).wait_recv()
+
+    def drain(self, pending=None):
+        for whole, slot in list(self.pending) if pending is None else pending:
+            self.copy(whole, slot, self.device).wait_send()
+            self.pending.remove((whole, slot))
+
+
+def gather(links, raw, vector, at, ready, order):
     x, y, z, core = at
     mate = device_of(x, y, z, 1 - core)
     squares = jnp.zeros((ROWS, TILE), F32)
@@ -155,46 +157,40 @@
     def along_y(step):
         return device_of(x, wrap(y + step), z, core)
 
-    def exchange(along, mine, theirs):
-        slots = [links.slot() for _ in range(1, 4)]
+    def exchange(along, mine, three):
+        slot = links.slot(three)
         for d in (2, 1, 3):
-            links.send(mine, slots[d - 1], along(d))
-
-        def wait():
-            for d in (1, 3, 2):
-                links.arrived(theirs(4 - d), slots[d - 1], along(4 - d))
-
-        return wait
-
-    near, far, handed = [], [], []
-    for begin, end in ZGROUPS:
-        for k in range(begin, end):
-            ready(k)
+            links.send(mine, slot, along(d))
+        return lambda: links.arrived(three, slot)
+
+    others = pl.ds(0, 3)
+    state = [None] * len(ZGROUPS)
+    for event, i in order:
+        begin, end = ZGROUPS[i]
         g = pl.ds(begin, end - begin)
-        near.append(
-            (
-                exchange(along_y, raw.at[0, core, x, y, g], lambda d, g=g: raw.at[0, core, x, wrap(y + d), g]),
-                exchange(along_x, raw.at[1, core, x, y, g], lambda d, g=g: raw.at[1, core, wrap(x + d), y, g]),
+        if event == "near":
+            ready(begin, end)
+            state[i] = (
+                exchange(along_y, raw.at[0, core, x, y, g], raw.at[0, core, x, others, g]),
+                exchange(along_x, raw.at[1, core, x, y, g], raw.at[1, core, others, y, g]),
             )
-        )
-    for (begin, end), (wait_y, wait_x) in zip(ZGROUPS, near):
-        g = pl.ds(begin, end - begin)
-        wait_y()
-        wait_first = exchange(along_x, raw.at[0, core, x, :, g], lambda d, g=g: raw.at[0, core, wrap(x + d), :, g])
-        wait_x()
-        wait_second = exchange(along_y, raw.at[1, core, :, y, g], lambda d, g=g: raw.at[1, core, :, wrap(y + d), g])
-        far.append((wait_first, wait_second))
-    for (begin, end), waits in zip(ZGROUPS, far):
-        g = pl.ds(begin, end - begin)
-        for wait in waits:
-            wait()
-        slot = links.slot()
-        links.send(raw.at[:, core, :, :, g], slot, mate)
-        handed.append(slot)
-        squares = settle(raw, vector, z, core, begin, end, squares)
-    for (begin, end), slot in zip(ZGROUPS, handed):
-        links.arrived(raw.at[:, 1 - core, :, :, pl.ds(begin, end - begin)], slot, mate)
-        squares = settle(raw, vector, z, 1 - core, begin, end, squares)
+        elif event == "far":
+            wait_y, wait_x = state[i]
+            wait_y()
+            first = exchange(along_x, raw.at[0, core, x, :, g], raw.at[0, core, others, :, g])
+            wait_x()
+            second = exchange(along_y, raw.at[1, core, :, y, g], raw.at[1, core, :, others, g])
+            state[i] = (first, second)
+        elif event == "hand":
+            for wait in state[i]:
+                wait()
+            here = raw.at[:, core, :, :, g]
+            state[i] = links.slot(here)
+            links.send(here, state[i], mate)
+            squares = settle(raw, vector, z, core, begin, end, squares)
+        else:
+            links.arrived(raw.at[:, 1 - core, :, :, g], state[i])
+            squares = settle(raw, vector, z, 1 - core, begin, end, squares)
     return squares
 
 
@@ -218,14 +214,17 @@
 
 def along_z(links, mine, place, at):
     x, y, z, core = at
-    slots = [links.slot() for _ in OFFSETS]
+    slots = [links.slot(place(pl.ds(max(begin, 1), end - max(begin, 1)))) if end > 1 else None for begin, end in ZGROUPS]
+    group = [i for i, (begin, end) in enumerate(ZGROUPS) for _ in range(begin, end)]
     for k in (7, 5, 6, 3, 4, 1, 2):
-        links.send(mine, slots[k], device_of(x, y, lax.rem(z - OFFSETS[k] + NZ, NZ), core), place(k))
-
-    def wait(k):
-        if k:
-            origin = lax.rem(z + (OFFSETS[k] + NZ), NZ)
-            links.arrived(place(k), slots[k], device_of(x, y, origin, core))
+        to = device_of(x, y, lax.rem(z - OFFSETS[k] + NZ, NZ), core)
+        links.send(mine, slots[group[k]], to, place(k))
+
+    def wait(begin, end):
+        slot = slots[group[begin]]
+        if slot is not None:
+            begin = max(begin, 1)
+            links.arrived(place(pl.ds(begin, end - begin)), slot)
 
     return wait
 
@@ -235,33 +234,30 @@
         rows = [total[h * 2 + k].reshape(N_TERM, ROWS, TILE) for k in range(2)]
         both = jnp.stack(rows, axis=1).reshape(N_TERM, 2 * ROWS, TILE).astype(BF16)
         out[:, h] = both
-    slots = [links.slot() for _ in range(1, N_TERM)]
-    for d in range(1, N_TERM):
+    peers = pl.ds(1, N_TERM - 1)
+    slot = links.slot(back.at[peers])
+    for d in sorted(range(1, N_TERM), key=lambda d: abs(d - N_TERM // 2)):
         peer = lax.rem(me + d, N_TERM)
-        links.send(out.at[peer], slots[d - 1], at_term(peer), back.at[d])
-    return slots
-
-
-def merge(links, slots, out, back, me, at_term):
-    acc = out[me].astype(F32)
-    for d in range(1, N_TERM):
-        peer = lax.rem(me - d + N_TERM, N_TERM)
-        links.arrived(back.at[d], slots[d - 1], at_term(peer))
-        acc = acc + back[d].astype(F32)
-    return acc.reshape(BLK, ROWS, TILE)
+        links.send(out.at[peer], slot, at_term(peer), back.at[d])
+
+    def wait():
+        acc = out[me].astype(F32)
+        links.arrived(back.at[peers], slot)
+        return (acc + jnp.sum(back[peers].astype(F32), axis=0)).reshape(BLK, ROWS, TILE)
+
+    return wait
 
 
 def everyone(links, mine, back, here, n, at):
-    slots = [links.slot() for _ in range(1, n)]
-    for d in range(1, n):
-        links.send(mine, slots[d - 1], at(lax.rem(here + d, n)), back.at[d])
+    peers = pl.ds(1, n - 1)
+    slot = links.slot(back.at[peers])
+    for d in sorted(range(1, n), key=lambda d: abs(d - n // 2)):
+        links.send(mine, slot, at(lax.rem(here + d, n)), back.at[d])
 
     def wait():
         acc = mine[...]
-        for d in range(1, n):
-            links.arrived(back.at[d], slots[d - 1], at(lax.rem(here - d + n, n)))
-            acc = acc + back[d]
-        return acc
+        links.arrived(back.at[peers], slot)
+        return acc + jnp.sum(back[peers], axis=0)
 
     return wait
 
@@ -341,7 +337,8 @@
     barrier = pltpu.get_barrier_semaphore()
     greeted = [at_term(lax.rem(term + d, N_TERM)) for d in range(1, N_TERM)]
     greeted += [at_sector(lax.rem(sector + d, N_SECTOR)) for d in range(1, N_SECTOR)]
-    greeted += [(z * 2 + 1 - y_hi, x * 4 + (1 - y_lo) * 2 + core)]
+    chip = lax.div(sector, 2)
+    greeted += [(z * 2 + 1 - y_hi, lax.rem(chip + d, N_SECTOR // 2) * 2 + core) for d in range(1, N_SECTOR // 2)]
     for device in greeted:
         pl.semaphore_signal(barrier, inc=1, device_id=device, device_id_type=MESH)
 
@@ -357,7 +354,7 @@
     for h in range(2):
         raw_one[h, core, x, y, 0] = jnp.concatenate(start[h * 2 : h * 2 + 2], axis=0).astype(BF16)
 
-    links = Links(send_sem, recv_sem)
+    links = Links(send_sem, recv_sem, device_of(x, y, z, 1 - core))
     pl.semaphore_wait(barrier, len(greeted))
     arrived = along_z(links, raw_one.at[:, core, x, y, 0], lambda k: raw_one.at[:, core, x, y, k], at)
 
@@ -371,7 +368,7 @@
     for copy in copies:
         copy.start()
 
-    start_squares = jnp.sum(gather(links, raw_one, vector, at, arrived), keepdims=True)
+    start_squares = jnp.sum(gather(links, raw_one, vector, at, arrived, ORDER_ONE), keepdims=True)
     for copy in copies + fetches[6:]:
         copy.wait()
     contract(steps_s, last_s, vector, lefts, rights, prefix, total)
@@ -382,11 +379,13 @@
         tile = vector[sector * BLK + b].astype(F32).reshape(N_TERM, ROWS, TILE)
         overlap = overlap + jnp.sum(tile * total[b].reshape(N_TERM, ROWS, TILE), axis=0)
     part[0] = overlap
+    gathered = list(links.pending)
     sector_sum = everyone(links, part.at[0], part_sector, sector, N_SECTOR, at_sector)
-    slots = spread(links, total, out_one, back_one, term, at_term)
+    rows_sum = spread(links, total, out_one, back_one, term, at_term)
     part[1] = sector_sum()
     term_sum = everyone(links, part.at[1], part_term, term, N_TERM, at_term)
-    coupled = merge(links, slots, out_one, back_one, term, at_term)
+    links.drain(gathered)
+    coupled = rows_sum()
     sigma = [jnp.where(inside[b], diag[b] * start[b] + coupled[b], 0.0) for b in range(BLK)]
     for b in range(BLK):
         rows_f32[0, b] = sigma[b]
@@ -395,22 +394,36 @@
         sigma_one[b] = sigma[b]
     rayleigh = jnp.sum(term_sum(), keepdims=True) / start_squares
 
-    def residual_here(k):
-        arrived_f32(k)
-        for h in range(2):
-            before = raw_one[h, core, x, y, k].astype(F32)
-            after = rows_f32[k, h * 2 : h * 2 + 2].reshape(2 * ROWS, TILE)
-            raw_two[h, core, x, y, k] = (after - rayleigh * before).astype(BF16)
-
-    squares = jnp.sum(gather(links, raw_two, vector, at, residual_here), keepdims=True)
+    def residual_here(begin, end):
+        arrived_f32(begin, end)
+        for k in range(begin, end):
+            for h in range(2):
+                before = raw_one[h, core, x, y, k].astype(F32)
+                after = rows_f32[k, h * 2 : h * 2 + 2].reshape(2 * ROWS, TILE)
+                raw_two[h, core, x, y, k] = (after - rayleigh * before).astype(BF16)
+
+    squares = jnp.sum(gather(links, raw_two, vector, at, residual_here, ORDER_TWO), keepdims=True)
     scale = lax.rsqrt(squares / float(NBLK * TILE * TILE) + 1e-06)
     contract(steps_s, last_s, vector, lefts, rights, prefix, total)
-    slots = spread(links, total, out_two, back_two, term, at_term)
-    coupled = merge(links, slots, out_two, back_two, term, at_term)
+    gathered = list(links.pending)
+    rows_sum = spread(links, total, out_two, back_two, term, at_term)
+    links.drain(gathered)
+    coupled = rows_sum()
     for b in range(BLK):
         second = raw_two[b // 2, core, x, y, 0].astype(F32)[(b % 2) * ROWS : (b % 2 + 1) * ROWS]
         sigma_two[b] = jnp.where(inside[b], (diag[b] * second + coupled[b]) * scale, 0.0)
     links.drain()
+
+
+def keep_kernel(one, two, one_out, two_out, sem):
+    copies = [
+        pltpu.make_async_copy(one, one_out, sem.at[0]),
+        pltpu.make_async_copy(two, two_out, sem.at[1]),
+    ]
+    for copy in copies:
+        copy.start()
+    for copy in copies:
+        copy.wait()
 
 
 def body(psi, diag_energy, block_shape, *rest):
@@ -421,7 +434,7 @@
     raw = pltpu.VMEM((2, NCORE, NX, NY, NZ, 2 * ROWS, TILE), BF16)
     rows = pltpu.VMEM((N_TERM, 2, 2 * ROWS, TILE), BF16)
     slots = pltpu.VMEM((1, 1, PAIRS), I32)
-    return pl.pallas_call(
+    sums = pl.pallas_call(
         kernel,
         out_shape=(out, out),
         in_specs=[hbm, hbm, smem, hbm, hbm, hbm, hbm, hbm, hbm, smem],
@@ -461,6 +474,14 @@
         ),
         name="two_products",
     )(psi.reshape(2, 2 * ROWS, TILE), diag_energy.reshape(BLK * ROWS, TILE), block_shape.T, *rest)
+    return pl.pallas_call(
+        keep_kernel,
+        out_shape=(out, out),
+        in_specs=[hbm, hbm],
+        out_specs=(hbm, hbm),
+        scratch_shapes=[pltpu.SemaphoreType.DMA((2,))],
+        name="keep",
+    )(*sums)
 
 
 def solution(mesh):

time: 79.5 us -> 71.5 us (0.90)
  Pallas kernels: 76.1 us -> 70.1 us
  local copies, waits for them, and re-layouts: 1.94 us -> 0 us
    pallas_call x1, Pallas kernels: 76.1 us -> 68 us  [body(): pl.pallas_call(kernel, out_shape=(out, out), in_specs=[hbm, hbm, smem, hb...]
    pallas_call x0 -> x1, Pallas kernels: none -> 2.11 us  [body(): pl.pallas_call(keep_kernel, out_shape=(out, out), in_specs=[hbm, hbm], ou...]
    unnamed x4 -> x0, local copies, waits for them, and re-layouts: 1.94 us -> none
where the time goes in v3:
time: 71.5 us; the launch traced here: 71.4 us
  Pallas kernels  70.1 us (98%)
  between operations  1.29 us (2%)
    pallas_call x1, Pallas kernels, body(): pl.pallas_call(kernel, out_shape=(out, out), in_specs=[hbm, hbm, smem, hb...  68 us
    pallas_call x1, Pallas kernels, body(): pl.pallas_call(keep_kernel, out_shape=(out, out), in_specs=[hbm, hbm], ou...  2.11 us

profile of v3, /device:TPU:1, one launch (start us, length us, event | category | flops | bytes accessed | tf_op | source)
XLA Modules:
  0.0 71.4 jit_solution(8234382161726384567)
XLA Ops:
  1.3 68.0 %two_products.1 = (f32[4,8,128]{2,1,0:T(8,128)}, f32[4,8,128]{2,1,0:T(8,128)}) custom-call(bf16[2,16,128]{2,1,0:T(8,128)(2,1)} %bitcast.4, f32[32,128]{1,0:T(8,128)} %bitcast.3, s32[2,4]{1,0:T(2,128)} %bitcast.5, bf16[1,1,32,128,128]{4,3,2,1,0:T(8,128)(2,1)} %env_left.1, bf16[1,1,32,128,128]{4,3,2,1,0:T(8,128)(2,1)} %env_right.1, s32[1,1,384]{2,1,0:T(1,128)} %source_hbm.1, ...), custom_call_target="tpu_custom_call" | custom-call | tf_op jit(solution)/shard_map/two_products/pallas_call | solution.py:437
  69.3 2.1 %keep.1 = (f32[4,8,128]{2,1,0:T(8,128)}, f32[4,8,128]{2,1,0:T(8,128)}) custom-call(f32[4,8,128]{2,1,0:T(8,128)} %get-tuple-element.4.one, f32[4,8,128]{2,1,0:T(8,128)} %get-tuple-element.5.two), custom_call_target="tpu_custom_call" | custom-call | tf_op jit(solution)/shard_map/keep/pallas_call | solution.py:477

commit v4 on v3

--- a/solution.py
+++ b/solution.py
@@ -21,19 +21,19 @@
 N_TERM, N_SECTOR = 16, 16
 NBLK = N_SECTOR * BLK
 GROUPS = ENV * BLK
-UNROLL = 96
+UNROLL = 192
 N_SEND = 64
 OFFSETS = (0, 1, -1, 2, -2, 3, -3, 4)
 ZGROUPS = ((0, 1), (1, 3), (3, 5), (5, 7), (7, 8))
 
 
 def order_of(*marks):
-    names = {"n": "near", "f": "far", "h": "hand", "t": "take"}
+    names = {"n": "near", "f": "far", "h": "hand", "t": "take", "a": "aside"}
     return tuple((names[mark[0]], int(mark[1:])) for mark in marks)
 
 
 ENDS = ("h0", "h1", "t0", "h2", "t1", "h3", "t2", "h4", "t3", "t4")
-ORDER_ONE = order_of("n0", "n1", "n2", "f0", "n3", "n4", "f1", "f2", "f3", "f4", *ENDS)
+ORDER_ONE = order_of("n0", "a0", "n1", "n2", "f0", "n3", "n4", "f1", "f2", "f3", "f4", *ENDS)
 ORDER_TWO = order_of("n0", "n1", "n2", "n3", "n4", "f0", "f1", "f2", "f3", "f4", *ENDS)
 NT = (((1,), (1,)), ((), ()))
 
@@ -143,7 +143,7 @@
             self.pending.remove((whole, slot))
 
 
-def gather(links, raw, vector, at, ready, order):
+def gather(links, raw, vector, at, ready, order, aside=None):
     x, y, z, core = at
     mate = device_of(x, y, z, 1 - core)
     squares = jnp.zeros((ROWS, TILE), F32)
@@ -168,7 +168,9 @@
     for event, i in order:
         begin, end = ZGROUPS[i]
         g = pl.ds(begin, end - begin)
-        if event == "near":
+        if event == "aside":
+            aside()
+        elif event == "near":
             ready(begin, end)
             state[i] = (
                 exchange(along_y, raw.at[0, core, x, y, g], raw.at[0, core, x, others, g]),
@@ -358,17 +360,19 @@
     pl.semaphore_wait(barrier, len(greeted))
     arrived = along_z(links, raw_one.at[:, core, x, y, 0], lambda k: raw_one.at[:, core, x, y, k], at)
 
-    for fetch in fetches[2:6]:
-        fetch.wait()
-    schedule(source[0], target[0], left[0], right[0], count[0, 0], steps_v, last_v)
     copies = [
         pltpu.make_async_copy(steps_v, steps_s, local_sem.at[8]),
         pltpu.make_async_copy(last_v, last_s, local_sem.at[9]),
     ]
-    for copy in copies:
-        copy.start()
-
-    start_squares = jnp.sum(gather(links, raw_one, vector, at, arrived, ORDER_ONE), keepdims=True)
+
+    def plan():
+        for fetch in fetches[2:6]:
+            fetch.wait()
+        schedule(source[0], target[0], left[0], right[0], count[0, 0], steps_v, last_v)
+        for copy in copies:
+            copy.start()
+
+    start_squares = jnp.sum(gather(links, raw_one, vector, at, arrived, ORDER_ONE, plan), keepdims=True)
     for copy in copies + fetches[6:]:
         copy.wait()
     contract(steps_s, last_s, vector, lefts, rights, prefix, total)
@@ -415,15 +419,9 @@
     links.drain()
 
 
-def keep_kernel(one, two, one_out, two_out, sem):
-    copies = [
-        pltpu.make_async_copy(one, one_out, sem.at[0]),
-        pltpu.make_async_copy(two, two_out, sem.at[1]),
-    ]
-    for copy in copies:
-        copy.start()
-    for copy in copies:
-        copy.wait()
+def keep_kernel(one, two, one_out, two_out):
+    one_out[...] = one[...]
+    two_out[...] = two[...]
 
 
 def body(psi, diag_energy, block_shape, *rest):
@@ -477,9 +475,8 @@
     return pl.pallas_call(
         keep_kernel,
         out_shape=(out, out),
-        in_specs=[hbm, hbm],
-        out_specs=(hbm, hbm),
-        scratch_shapes=[pltpu.SemaphoreType.DMA((2,))],
+        in_specs=[vmem, vmem],
+        out_specs=(vmem, vmem),
         name="keep",
     )(*sums)
 

time: 71.5 us -> 70 us (0.979)
  Pallas kernels: 70.1 us -> 68.5 us
    pallas_call x1, Pallas kernels: 68 us -> 67.1 us  [body(): pl.pallas_call(kernel, out_shape=(out, out), in_specs=[hbm, hbm, smem, hb...]
    pallas_call x1, Pallas kernels: 2.11 us -> 1.35 us  [body(): pl.pallas_call(keep_kernel, out_shape=(out, out), in_specs=[vmem, vmem],...]
where the time goes in v4:
time: 70 us; the launch traced here: 69.8 us
  Pallas kernels  68.5 us (98%)
  between operations  1.29 us (2%)
    pallas_call x1, Pallas kernels, body(): pl.pallas_call(kernel, out_shape=(out, out), in_specs=[hbm, hbm, smem, hb...  67.1 us

profile of v4, /device:TPU:1, one launch (start us, length us, event | category | flops | bytes accessed | tf_op | source)
XLA Modules:
  0.0 69.8 jit_solution(448619315210058422)
XLA Ops:
  1.3 67.1 %two_products.1 = (f32[4,8,128]{2,1,0:T(8,128)}, f32[4,8,128]{2,1,0:T(8,128)}) custom-call(bf16[2,16,128]{2,1,0:T(8,128)(2,1)} %bitcast.4, f32[32,128]{1,0:T(8,128)} %bitcast.3, s32[2,4]{1,0:T(2,128)} %bitcast.5, bf16[1,1,32,128,128]{4,3,2,1,0:T(8,128)(2,1)} %env_left.1, bf16[1,1,32,128,128]{4,3,2,1,0:T(8,128)(2,1)} %env_right.1, s32[1,1,384]{2,1,0:T(1,128)} %source_hbm.1, ...), custom_call_target="tpu_custom_call" | custom-call | tf_op jit(solution)/shard_map/two_products/pallas_call | solution.py:435
  68.4 1.3 %keep.1 = (f32[4,8,128]{2,1,0:T(8,128)}, f32[4,8,128]{2,1,0:T(8,128)}) custom-call(f32[4,8,128]{2,1,0:T(8,128)} %get-tuple-element.4.one, f32[4,8,128]{2,1,0:T(8,128)} %get-tuple-element.5.two), custom_call_target="tpu_custom_call" | custom-call | tf_op jit(solution)/shard_map/keep/pallas_call | solution.py:475

commit v5 on v4

--- a/solution.py
+++ b/solution.py
@@ -21,7 +21,7 @@
 N_TERM, N_SECTOR = 16, 16
 NBLK = N_SECTOR * BLK
 GROUPS = ENV * BLK
-UNROLL = 192
+UNROLL = 384
 N_SEND = 64
 OFFSETS = (0, 1, -1, 2, -2, 3, -3, 4)
 ZGROUPS = ((0, 1), (1, 3), (3, 5), (5, 7), (7, 8))
@@ -218,7 +218,7 @@
     x, y, z, core = at
     slots = [links.slot(place(pl.ds(max(begin, 1), end - max(begin, 1)))) if end > 1 else None for begin, end in ZGROUPS]
     group = [i for i, (begin, end) in enumerate(ZGROUPS) for _ in range(begin, end)]
-    for k in (7, 5, 6, 3, 4, 1, 2):
+    for k in range(1, NZ):
         to = device_of(x, y, lax.rem(z - OFFSETS[k] + NZ, NZ), core)
         links.send(mine, slots[group[k]], to, place(k))
 
@@ -333,7 +333,7 @@
             )
         )
     ]
-    for fetch in fetches:
+    for fetch in fetches[:2]:
         fetch.start()
 
     barrier = pltpu.get_barrier_semaphore()
@@ -343,6 +343,8 @@
     greeted += [(z * 2 + 1 - y_hi, lax.rem(chip + d, N_SECTOR // 2) * 2 + core) for d in range(1, N_SECTOR // 2)]
     for device in greeted:
         pl.semaphore_signal(barrier, inc=1, device_id=device, device_id_type=MESH)
+    for fetch in fetches[2:]:
+        fetch.start()
 
     row = lax.broadcasted_iota(I32, (ROWS, TILE), 0) + term * ROWS
     col = lax.broadcasted_iota(I32, (ROWS, TILE), 1)

time: 70 us -> 68.1 us (0.973)
  Pallas kernels: 68.5 us -> 66.6 us
    pallas_call x1, Pallas kernels: 67.1 us -> 65.2 us  [body(): pl.pallas_call(kernel, out_shape=(out, out), in_specs=[hbm, hbm, smem, hb...]
where the time goes in v5:
time: 68.1 us; the launch traced here: 67.9 us
  Pallas kernels  66.6 us (98%)
  between operations  1.29 us (2%)
    pallas_call x1, Pallas kernels, body(): pl.pallas_call(kernel, out_shape=(out, out), in_specs=[hbm, hbm, smem, hb...  65.2 us

profile of v5, /device:TPU:1, one launch (start us, length us, event | category | flops | bytes accessed | tf_op | source)
XLA Modules:
  0.0 67.9 jit_solution(4284800972098722658)
XLA Ops:
  1.3 65.2 %two_products.1 = (f32[4,8,128]{2,1,0:T(8,128)}, f32[4,8,128]{2,1,0:T(8,128)}) custom-call(bf16[2,16,128]{2,1,0:T(8,128)(2,1)} %bitcast.4, f32[32,128]{1,0:T(8,128)} %bitcast.3, s32[2,4]{1,0:T(2,128)} %bitcast.5, bf16[1,1,32,128,128]{4,3,2,1,0:T(8,128)(2,1)} %env_left.1, bf16[1,1,32,128,128]{4,3,2,1,0:T(8,128)(2,1)} %env_right.1, s32[1,1,384]{2,1,0:T(1,128)} %source_hbm.1, ...), custom_call_target="tpu_custom_call" | custom-call | tf_op jit(solution)/shard_map/two_products/pallas_call | solution.py:437
  66.5 1.3 %keep.1 = (f32[4,8,128]{2,1,0:T(8,128)}, f32[4,8,128]{2,1,0:T(8,128)}) custom-call(f32[4,8,128]{2,1,0:T(8,128)} %get-tuple-element.4.one, f32[4,8,128]{2,1,0:T(8,128)} %get-tuple-element.5.two), custom_call_target="tpu_custom_call" | custom-call | tf_op jit(solution)/shard_map/keep/pallas_call | solution.py:477

commit v6 on v5

--- a/solution.py
+++ b/solution.py
@@ -434,9 +434,10 @@
     raw = pltpu.VMEM((2, NCORE, NX, NY, NZ, 2 * ROWS, TILE), BF16)
     rows = pltpu.VMEM((N_TERM, 2, 2 * ROWS, TILE), BF16)
     slots = pltpu.VMEM((1, 1, PAIRS), I32)
+    held = pltpu.VMEM((BLK, ROWS, TILE), F32)
     sums = pl.pallas_call(
         kernel,
-        out_shape=(out, out),
+        out_shape=(held, held),
         in_specs=[hbm, hbm, smem, hbm, hbm, hbm, hbm, hbm, hbm, smem],
         out_specs=(vmem, vmem),
         scratch_shapes=[
@@ -480,7 +481,7 @@
         in_specs=[vmem, vmem],
         out_specs=(vmem, vmem),
         name="keep",
-    )(*sums)
+    )(*[pltpu.with_memory_space_constraint(each, pltpu.VMEM) for each in sums])
 
 
 def solution(mesh):

time: 68.1 us -> 66.7 us (0.979)
  Pallas kernels: 66.6 us -> 65.3 us
    pallas_call x1, Pallas kernels: 1.35 us -> 0.61 us  [body(): pl.pallas_call(keep_kernel, out_shape=(out, out), in_specs=[vmem, vmem],...]
where the time goes in v6:
time: 66.7 us; the launch traced here: 66.5 us
  Pallas kernels  65.3 us (98%)
  between operations  1.29 us (2%)
    pallas_call x1, Pallas kernels, body(): pl.pallas_call(kernel, out_shape=(held, held), in_specs=[hbm, hbm, smem,...  64.6 us

profile of v6, /device:TPU:1, one launch (start us, length us, event | category | flops | bytes accessed | tf_op | source)
XLA Modules:
  0.0 66.5 jit_solution(16998455855313074256)
XLA Ops:
  1.3 64.6 %two_products.1 = (f32[4,8,128]{2,1,0:T(8,128)S(1)}, f32[4,8,128]{2,1,0:T(8,128)S(1)}) custom-call(bf16[2,16,128]{2,1,0:T(8,128)(2,1)} %bitcast.4, f32[32,128]{1,0:T(8,128)} %bitcast.3, s32[2,4]{1,0:T(2,128)} %bitcast.5, bf16[1,1,32,128,128]{4,3,2,1,0:T(8,128)(2,1)} %env_left.1, bf16[1,1,32,128,128]{4,3,2,1,0:T(8,128)(2,1)} %env_right.1, ...), custom_call_target="tpu_custom_call" | custom-call | tf_op jit(solution)/shard_map/two_products/pallas_call | solution.py:438
  65.9 0.6 keep.1
